TPU v7x, 128 devices: a whole 4x4x4 slice. The times are simulated.
128 devices in a mesh: tok: 4 (over y), vocab: 32 (over x, z, core).
Axes of the slice: x: 4, y: 4, z: 4, core: 2. Of those that a mesh axis runs over, the one named last changes fastest.
Arguments:
- teacher_logits: bfloat16 [512, 131072], P('tok', 'vocab'), may hold values from -18 to 240
- hidden: bfloat16 [512, 4608], P('tok'), may hold values from -6 to 6
- new_head: bfloat16 [4608, 131072], P(None, ('tok', 'vocab')), may hold values from -0.26516504 to 0.26516504
- labels: int32 [512], replicated, may hold values from 0 to 131071
- map_target: int32 [1024, 4], P('vocab'), may hold values from 0 to 1023, as said below
- map_weight: bfloat16 [1024, 4, 128, 128], P('vocab'), may hold values from 0 to 0.017578125, as said below
Outputs:
- loss: float32 [512], P('tok')
- head_grad: bfloat16 [4608, 131072], P(None, ('tok', 'vocab'))
Inputs may be any that keep to these rules, and one draw needn't show every extreme that they name: `map_target`: values are ids of new blocks; new block b belongs to the device at index b // 8 of tok and vocab together, tok first. Of the 128 entries of one vocab index, at most 2 belong to one device, and some device gets exactly 2. `map_weight`: entries are non-negative.
All inputs are finite; a program needn't handle non-finite values.
Results may differ from a plain program's by a relative error of at most 0.001.
The roundings to bfloat16 on the way count: a program that leaves them out, or rounds other values in their place, can miss the bound.
Values may be sent and summed in bfloat16 or wider, within the bound.
A program may use at most 128 MiB of HBM per device.

v0:
```python
import jax
import jax.numpy as jnp
from jax import lax
from jax.sharding import PartitionSpec as P


def local(teacher_logits, hidden, new_head, labels, map_target, map_weight):
    tok_rows = teacher_logits.shape[0]
    block = map_weight.shape[2]
    fanout = map_weight.shape[1]
    old_blocks = map_target.shape[0]
    entries = old_blocks * fanout
    n_tok = lax.axis_size("tok")
    n_vocab = lax.axis_size("vocab")
    nodes = n_tok * n_vocab
    capacity = max(2, 2 * entries // nodes)
    new_cols = new_head.shape[1]
    per_node = new_cols // block
    own_index = lax.axis_index(("tok", "vocab"))
    scores = teacher_logits.astype(jnp.float32)
    local_top = jnp.max(scores, axis=1)
    highest = lax.pmax(local_top, "vocab")
    total = lax.psum(jnp.sum(jnp.exp(scores - highest[:, None]), axis=1), "vocab")
    teacher_prob = (jnp.exp(scores - highest[:, None]) / total[:, None]).astype(jnp.bfloat16)
    pieces = teacher_prob.reshape(tok_rows, old_blocks, block)
    contrib = jnp.einsum("tjb,jkbc->jktc", pieces, map_weight, preferred_element_type=jnp.float32)
    contrib = contrib.astype(jnp.bfloat16).reshape(entries, tok_rows, block)
    owners = (map_target // per_node).reshape(entries)
    earlier = jnp.arange(entries)[None, :] < jnp.arange(entries)[:, None]
    slots = jnp.sum((owners[:, None] == owners[None, :]) & earlier, axis=1)
    outbox = (
        jnp.zeros((nodes, capacity, tok_rows, block), jnp.bfloat16).at[owners, slots].set(contrib)
    )
    inbox = lax.all_to_all(outbox, ("tok", "vocab"), split_axis=0, concat_axis=0, tiled=True)
    inbox = inbox.reshape(n_tok, n_vocab, capacity, tok_rows, block)
    targets_all = lax.all_gather(map_target, "vocab", axis=0, tiled=True).reshape(n_vocab, entries)
    owners_all = targets_all // per_node
    local_block = targets_all % per_node
    slots_all = jnp.sum((owners_all[:, :, None] == owners_all[:, None, :]) & earlier[None], axis=2)
    picked = (owners_all == own_index)[:, :, None] & (
        slots_all[:, :, None] == jnp.arange(capacity)[None, None, :]
    )
    block_hit = local_block[:, :, None] == jnp.arange(per_node)[None, None, :]
    landing = jnp.einsum(
        "vec,veb->vcb", picked.astype(jnp.float32), block_hit.astype(jnp.float32)
    ).astype(jnp.bfloat16)
    target = jnp.einsum("vcb,svctk->stbk", landing, inbox, preferred_element_type=jnp.float32)
    target = target.reshape(n_tok * tok_rows, new_cols)
    everyone = lax.all_gather(hidden, "tok", axis=0, tiled=True)
    logits = jnp.dot(everyone, new_head, preferred_element_type=jnp.float32)
    columns = own_index * new_cols + jnp.arange(new_cols, dtype=jnp.int32)
    label_hit = labels[:, None] == columns[None, :]
    label_part = jnp.sum(jnp.where(label_hit, logits, 0.0), axis=1)
    mass_part = jnp.sum(target, axis=1)
    inner_part = jnp.sum(target * logits, axis=1)
    row_top = jnp.max(logits, axis=1)
    top_all = lax.pmax(row_top, ("tok", "vocab"))
    exp_part = jnp.sum(jnp.exp(logits - top_all[:, None]), axis=1)
    total_all, target_mass, inner, label_logit = lax.psum(
        (exp_part, mass_part, inner_part, label_part), ("tok", "vocab")
    )
    log_total = top_all + jnp.log(total_all)
    loss_all = target_mass * log_total - inner + log_total - label_logit
    loss = lax.dynamic_slice_in_dim(loss_all, lax.axis_index("tok") * tok_rows, tok_rows)
    probs = jnp.exp(logits - log_total[:, None])
    grad_logits = (
        (target_mass + 1.0)[:, None] * probs - target - label_hit.astype(jnp.float32)
    ).astype(jnp.bfloat16)
    head_grad = lax.dot_general(
        everyone, grad_logits, (((0,), (0,)), ((), ())), preferred_element_type=jnp.float32
    )
    return (loss, head_grad.astype(jnp.bfloat16))


def solution(mesh):
    return jax.shard_map(
        local,
        mesh=mesh,
        in_specs=(
            P("tok", "vocab"),
            P("tok", None),
            P(None, ("tok", "vocab")),
            P(),
            P("vocab", None),
            P("vocab", None, None, None),
        ),
        out_specs=(P("tok"), P(None, ("tok", "vocab"))),
        check_vma=False,
    )
```

profile of v0, /device:TPU:1, one launch (start us, length us, event | category | flops | bytes accessed | tf_op | source)
XLA Modules:
  0.0 477.8 jit_solution(10782458382185194525)
XLA Ops:
  7.2 0.0 all-gather.3.cloned.1.call-start
  7.2 0.7 all-gather.3.cloned.1.call-update
  7.9 0.7 add_select_fusion.2
  8.6 0.1 copy.44
  8.7 0.1 eq.79
  8.8 0.1 reshape.176
  8.9 1.5 reduce_max.23
  10.4 64.8 %pmax.14 = f32[128]{0:T(128)S(1)} all-reduce(bf16[128]{0:T(256)(128)(2,1)S(1)} %reduce_max.23), channel_id=1, replica_groups=mesh['tok'=4,'vocab'=32] {'vocab'}, use_global_device_ids=true, to_apply=%region_2.0 | all-reduce | flops 128 | bytes 768 | tf_op jit(solution)/shard_map/pmax | solution.py:22
  75.2 0.5 fusion.7
  75.7 67.0 %psum.35 = f32[128]{0:T(128)S(1)} all-reduce(f32[128]{0:T(128)S(1)} %fusion.7), channel_id=1, replica_groups=mesh['tok'=4,'vocab'=32] {'vocab'}, use_global_device_ids=true, to_apply=%region_4.5 | all-reduce | flops 128 | bytes 1024 | tf_op jit(solution)/shard_map/psum | solution.py:23
  142.7 0.5 fusion.9
  143.2 0.2 copy.62
  143.5 0.2 convert_reduce_fusion.1
  143.6 1.3 copy-done.2
  144.9 3.2 convolution_convert_fusion.1
  148.1 5.5 %broadcast_in_dim.5 = bf16[128,2,128,128]{3,2,1,0:T(8,128)(2,1)} broadcast(bf16[]{:T(256)} %constant.50.clone.1), dimensions={} | broadcast | bytes 8388610 | tf_op jit(solution)/shard_map/broadcast_in_dim | solution.py:32
  153.6 20.7 %scatter_fusion = bf16[128,2,128,128]{3,2,1,0:T(8,128)(2,1)} fusion(bf16[128,2,128,128]{3,2,1,0:T(8,128)(2,1)} %broadcast_in_dim.5, s32[128]{0:T(128)S(1)} %fusion.26, bf16[128,128,128]{2,1,0:T(8,128)(2,1)} %bitcast.43), kind=kCustom, calls=%fused_computation | custom fusion | bytes 12583936 | tf_op jit(solution)/shard_map/scatter | solution.py:32
  174.4 5.4 %all-to-all-start = ((bf16[128,2,128,128]{3,2,1,0:T(8,128)(2,1)}), bf16[128,2,128,128]{3,2,1,0:T(8,128)(2,1)}, u32[]{:S(2)}, u32[]{:S(2)}) async-start(bf16[128,2,128,128]{3,2,1,0:T(8,128)(2,1)} %scatter_fusion), calls=%async_computation | async-start | bytes 16777216 | tf_op jit(solution)/shard_map/all_to_all | solution.py:34
  179.8 117.2 %all-gather = s32[32,32,4]{1,2,0:T(4,128)S(1)} all-gather(s32[1,32,4]{1,2,0:T(4,128)S(1)} %bitcast.47), channel_id=1, replica_groups=mesh['tok'=4,'vocab'=32] {'vocab'}, dimensions={0}, use_global_device_ids=true | all-gather | bytes 16896 | tf_op jit(solution)/shard_map/all_gather | solution.py:36
  297.0 0.1 copy.47
  297.1 0.1 copy.48
  297.2 1.3 convert_reduce_fusion
  298.5 0.2 fusion.8
  298.7 0.0 all-gather.3.cloned.1.call-done
  298.7 10.1 %fusion.27 = (f32[512]{0:T(512)S(1)}, f32[512,1024]{1,0:T(8,128)}) fusion(bf16[512,4608]{1,0:T(8,128)(2,1)} %all-gather.3.cloned.1.call-done, bf16[4608,1024]{1,0:T(8,128)(2,1)} %param.8), kind=kOutput, calls=%fused_computation.64 | convolution fusion | flops 4832361984 | bytes 16254976 | tf_op jit(solution)/shard_map/dot_general | solution.py:50
  308.8 65.0 %pmax.15 = f32[512]{0:T(512)S(1)} all-reduce(f32[512]{0:T(512)S(1)} %get-tuple-element.24), channel_id=1, replica_groups=mesh['tok'=4,'vocab'=32] {'tok','vocab'}, use_global_device_ids=true, to_apply=%region_10.11 | all-reduce | flops 512 | bytes 4096 | tf_op jit(solution)/shard_map/pmax | solution.py:57
  373.9 8.9 %bitcast_reduce_fusion = (f32[4,128]{1,0:T(4,128)S(1)}, f32[4,128,128,8,1]{2,3,4,1,0:T(8,128)S(1)}) fusion(bf16[32,2,8,1,1]{2,1,0,4,3:T(2,128)(2,1)S(1)} %fusion.8, bf16[4,32,2,128,128]{4,3,2,1,0:T(8,128)(2,1)} %bitcast.5), kind=kOutput, calls=%fused_computation.14 | convolution fusion | flops 67632640 | bytes 10488832 | tf_op jit(solution)/shard_map/vcb,svctk->stbk/dot_general | solution.py:47
  382.8 1.2 fusion.6
  384.0 62.9 %all-reduce = (f32[512]{0:T(512)S(1)}, f32[512]{0:T(512)S(1)}, f32[512]{0:T(512)S(1)}, f32[512]{0:T(512)S(1)}) all-reduce(f32[512]{0:T(512)S(1)} %get-tuple-element.13, f32[512]{0:T(512)S(1)} %get-tuple-element.14, f32[512]{0:T(512)S(1)} %get-tuple-element.12, f32[512]{0:T(512)S(1)} %bitcast.46), channel_id=1, replica_groups=mesh['tok'=4,'vocab'=32] {'tok','vocab'}, use_global_device_ids=true, to_apply=%region_16.17 | all-reduce | flops 2048 | bytes 16384 | tf_op jit(solution)/shard_map/psum | solution.py:59
  446.8 10.9 %fusion.2 = bf16[4608,1024]{0,1:T(8,128)(2,1)} fusion(bf16[512,4608]{1,0:T(8,128)(2,1)} %all-gather.3.cloned.1.call-done, f32[512,1024]{1,0:T(8,128)} %get-tuple-element.25, f32[64,8,8,128]{3,2,1,0:T(8,128)S(1)} %bitcast.42, f32[512]{0:T(512)S(1)} %get-tuple-element.20, f32[512]{0:T(512)S(1)} %get-tuple-element.23, s32[1024]{0:T(1024)S(1)} %iota_add_fusion, ...), kind=kOutput, calls=%fused_computation.4 | convolution fusion | flops 4840226816 | bytes 18360320 | tf_op jit(solution)/shard_map/dot_general | solution.py:69
  457.8 12.6 %copy.54 = bf16[4608,1024]{1,0:T(8,128)(2,1)} copy(bf16[4608,1024]{0,1:T(8,128)(2,1)} %fusion.2) | data formatting | bytes 18874368
  470.4 0.6 dynamic_slice.3
  (16 shorter events, 0.1 us)
Async XLA Ops:
  7.2 68.0 %copy-start = (bf16[128,4096]{1,0:T(8,128)(2,1)S(1)}, bf16[128,4096]{1,0:T(8,128)(2,1)}, u32[]{:S(2)}) copy-start(bf16[128,4096]{1,0:T(8,128)(2,1)} %param.6) | copy-start | bytes 3145732
  7.2 291.5 %all-gather.3.cloned.1.call-start = ((), (), s32[]{:S(2)}) async-start(), calls=%async_computation.1 | async-start | bytes 5898240 | tf_op jit(solution)/shard_map/all_gather | solution.py:49
  142.7 2.2 copy-start.2
  174.4 5.4 %copy-start.4 = (s32[32,4]{0,1:T(4,128)S(1)}, s32[32,4]{0,1:T(4,128)}, u32[]{:S(2)}) copy-start(s32[32,4]{0,1:T(4,128)} %param.10) | copy-start | bytes 1540
  174.4 199.5 %all-to-all-start = ((bf16[128,2,128,128]{3,2,1,0:T(8,128)(2,1)}), bf16[128,2,128,128]{3,2,1,0:T(8,128)(2,1)}, u32[]{:S(2)}, u32[]{:S(2)}) async-start(bf16[128,2,128,128]{3,2,1,0:T(8,128)(2,1)} %scatter_fusion), calls=%async_computation | async-start | bytes 16777216 | tf_op jit(solution)/shard_map/all_to_all | solution.py:34
  373.8 8.9 %copy-start.1 = (f32[512,1024]{1,0:T(8,128)S(1)}, f32[512,1024]{1,0:T(8,128)}, u32[]{:S(2)}) copy-start(f32[512,1024]{1,0:T(8,128)} %get-tuple-element.25) | copy-start | bytes 6291460
  373.9 8.9 %copy-start.3 = (s32[512]{0:T(512)S(1)}, s32[512]{0:T(512)}, u32[]{:S(2)}) copy-start(s32[512]{0:T(512)} %param.9) | copy-start | bytes 6148
Sparse Core Ops, SparseCore 0:
  9.7 55.8 all-gather.2
where the time goes:
time: 479 us; the launch traced here: 478 us
  blocking collectives  377 us (79%)
  local copies, waits for them, and re-layouts  41.4 us (9%)
  matrix products  33.3 us (7%)
  between operations  14.2 us (3%)
  other arithmetic  5.87 us (1%)
  starting transfers between devices  5.46 us (1%)
    all_gather x1, blocking collectives, local(): lax.all_gather(map_target, 'vocab', axis=0, tiled=True)  117 us
    psum x1, blocking collectives, local(): lax.psum(jnp.sum(jnp.exp(scores - highest[:, None]), axis=1), 'vocab')  67 us
    pmax x1, blocking collectives, local(): top_all = lax.pmax(row_top, ('tok', 'vocab'))  65 us
    pmax x1, blocking collectives, local(): highest = lax.pmax(local_top, 'vocab')  64.8 us
    psum x1, blocking collectives, local(): lax.psum((exp_part, mass_part, inner_part, label_part), ('tok', 'vocab'))  62.9 us
    scatter x1, local copies, waits for them, and re-layouts, local(): jnp.zeros((nodes, capacity, tok_rows, block), jnp.bfloat16)  20.7 us
    unnamed x12, local copies, waits for them, and re-layouts  14.1 us
    dot_general x1, matrix products, local(): lax.dot_general(everyone, grad_logits, (((0,), (0,)), ((), ())), preferre...  10.9 us
  transfers between devices with their start and end apart: 2, of which 0 were waited for; matrix products, arithmetic and copies ran while one was open for 9% of the time, Pallas kernels for 0%

commit v1 on v0

v1 whole, which is shorter than its diff:
```python
import functools

import jax
import jax.numpy as jnp
from jax import lax
from jax.experimental import pallas as pl
from jax.experimental.pallas import tpu as pltpu
from jax.sharding import PartitionSpec as P

MESH = pl.DeviceIdType.MESH
F32 = jnp.float32
BF16 = jnp.bfloat16

NY = 4
NX = 4
NZ = 4
NC = 2
ROWS = 128
HALF = 64
BLK = 128
FAN = 4
D = 4608
HD = D // 2
VN = 1024
PER = 8
OLD = 32
ENT = OLD * FAN

FIRST = [(0, 1), (1, 0), (1, 1), (2, 0), (2, 1), (3, 0), (3, 1)]


def vocab_index(x, z, c):
    return (x * NZ + z) * NC + c


def as_row(column):
    return jnp.transpose(jnp.broadcast_to(column, (ROWS, BLK)))[0:1, :]


def as_column(row):
    return jnp.transpose(jnp.broadcast_to(row, (ROWS, BLK)))


def exchange_kernel(
    entry_ref, valid_ref, mask_ref, label_ref, raw_hbm, hidden_hbm, head_hbm, weight_hbm,
    loss_ref, grad_ref, everyone_hbm,
    raw, prob, weight, hidden, head, logits, out1, in1, out2, in2, masks, mass_acc,
    log_total, mass_plus, rest,
    t1_out, t1_in, t2_out, t2_in, t3_out, t3_in,
    a1_out, a1_in, a2_out, a2_in, a3_out, a3_in,
    f1_out, f1_in, f2_out, f2_in, f3_out, f3_in,
    local_sem, raw_send, raw_recv, mask_send, mask_recv, p1_send, p1_recv, p2_send, p2_recv,
    hid_send, hid_recv, sib_send, sib_recv,
    t1_send, t1_recv, t2_send, t2_recv, t3_send, t3_recv,
    a1_send, a1_recv, a2_send, a2_recv, a3_send, a3_recv,
    f1_send, f1_recv, f2_send, f2_recv, f3_send, f3_recv,
):
    y = lax.axis_index("tok")
    v = lax.axis_index("vocab")
    x = v // (NZ * NC)
    z = (v // NC) % NZ
    c = v % NC

    def remote(src, dst, send, recv, device):
        return pltpu.make_async_remote_copy(
            src_ref=src, dst_ref=dst, send_sem=send, recv_sem=recv,
            device_id=device, device_id_type=MESH,
        )

    def along_x(step, core_step=0):
        return (y, vocab_index((x + step) % NX, z, (c + core_step) % NC))

    def along_z(step, core_step=0):
        return (y, vocab_index(x, (z + step) % NZ, (c + core_step) % NC))

    def along_y(step):
        return ((y + step) % NY, v)

    load_raw = pltpu.make_async_copy(raw_hbm, raw.at[0], local_sem.at[0])
    load_weight = pltpu.make_async_copy(weight_hbm, weight, local_sem.at[1])
    own_rows = pl.ds(pl.multiple_of(y * ROWS, ROWS), ROWS)
    load_hidden = pltpu.make_async_copy(hidden_hbm, hidden.at[own_rows], local_sem.at[2])
    load_head = pltpu.make_async_copy(head_hbm, head, local_sem.at[3])
    load_raw.start()
    load_weight.start()
    load_hidden.start()
    load_head.start()

    barrier = pltpu.get_barrier_semaphore()
    partners = [along_x(da, dc) for da, dc in FIRST]
    partners += [along_z(da, dc) for da, dc in FIRST if da]
    partners += [along_y(step) for step in (1, 2, 3)]
    for partner in partners:
        pl.semaphore_signal(barrier, inc=1, device_id=partner, device_id_type=MESH)
    pl.semaphore_wait(barrier, len(partners))

    def first_partner(h, i):
        da, dc = FIRST[i]
        return along_x(da, dc) if h == 0 else along_z(da, dc)

    def mask_copy(h, i):
        da, dc = FIRST[i]
        c2 = (c + dc) % NC
        if h == 0:
            src = mask_ref.at[(x + da) % NX, :, c2]
        else:
            src = mask_ref.at[:, (z + da) % NZ, c2]
        return remote(src, masks.at[h, i], mask_send.at[h, i], mask_recv.at[h, i],
                      first_partner(h, i))

    def first_copy(g, h, i):
        da, dc = FIRST[i]
        c2 = (c + dc) % NC
        rows = pl.ds(h * HALF, HALF)
        if h == 0:
            src = out1.at[g, (x + da) % NX, :, c2, :, rows]
        else:
            src = out1.at[g, :, (z + da) % NZ, c2, :, rows]
        return remote(src, in1.at[g, h, i], p1_send.at[g, h, i], p1_recv.at[g, h, i],
                      first_partner(h, i))

    def second_copy(g, h, d):
        if h == 0:
            q, device = (z + d) % NZ, along_z(d)
        else:
            q, device = (x + d) % NX, along_x(d)
        return remote(out2.at[g, h, q], in2.at[g, h, d - 1], p2_send.at[g, h, d - 1],
                      p2_recv.at[g, h, d - 1], device)

    upper, lower = pl.ds(0, HALF), pl.ds(HALF, HALF)
    raw_copies = [
        remote(raw.at[0], raw.at[1], raw_send.at[0], raw_recv.at[0], along_y(1)),
        remote(raw.at[0], raw.at[3], raw_send.at[1], raw_recv.at[1], along_y(3)),
        remote(raw.at[1, upper], raw.at[2, upper], raw_send.at[2], raw_recv.at[2], along_y(1)),
        remote(raw.at[3, lower], raw.at[2, lower], raw_send.at[3], raw_recv.at[3], along_y(3)),
    ]

    own_columns = pl.ds(pl.multiple_of(c * HD, HD), HD)

    def rows_of(d):
        return pl.ds(pl.multiple_of(((y - d + NY) % NY) * ROWS, ROWS), ROWS)

    def hidden_copy(d):
        part = hidden.at[own_rows, own_columns]
        return remote(part, part, hid_send.at[d - 1], hid_recv.at[d - 1], along_y(d))

    def sibling_copy(d):
        part = hidden.at[rows_of(d), own_columns]
        return remote(part, part, sib_send.at[d - 1], sib_recv.at[d - 1], along_x(0, 1))

    def stage_x(out, into, send, recv):
        return [remote(out, into.at[i], send.at[i], recv.at[i], first_partner(0, i))
                for i in range(7)]

    def stage_z(out, into, send, recv):
        return [remote(out, into.at[d - 1], send.at[d - 1], recv.at[d - 1], along_z(d))
                for d in (1, 2, 3)]

    def stage_y(out, into, send, recv):
        return [remote(out, into.at[d - 1], send.at[d - 1], recv.at[d - 1], along_y(d))
                for d in (1, 2, 3)]

    pending = []

    def start(copies):
        for copy in copies:
            copy.start()
        pending.extend(copies)

    def arrived(copies):
        for copy in copies:
            copy.wait_recv()

    load_raw.wait()
    start(raw_copies[:2])
    mask_copies = [mask_copy(h, i) for h in (0, 1) for i in range(7)]
    start(mask_copies)

    def block_max(j, acc):
        part = raw[0, :, pl.ds(pl.multiple_of(j * BLK, BLK), BLK)].astype(F32)
        return jnp.maximum(acc, part)

    top = lax.fori_loop(1, OLD, block_max, raw[0, :, pl.ds(0, BLK)].astype(F32), unroll=4)
    top = jnp.broadcast_to(jnp.max(top, axis=1, keepdims=True), (ROWS, BLK))

    def block_sum(j, acc):
        part = raw[0, :, pl.ds(pl.multiple_of(j * BLK, BLK), BLK)].astype(F32)
        return acc + jnp.exp(part - top)

    total = lax.fori_loop(0, OLD, block_sum, jnp.zeros((ROWS, BLK), F32), unroll=4)
    total = jnp.sum(total, axis=1, keepdims=True)
    sublane = lax.broadcasted_iota(jnp.int32, (8, BLK), 0)

    def stacked(first, second):
        return jnp.where(sublane == 0, jnp.broadcast_to(first, (8, BLK)),
                         jnp.broadcast_to(second, (8, BLK)))

    def joined(pairs):
        best = functools.reduce(jnp.maximum, [p[0:1] for p in pairs])
        mass = functools.reduce(jnp.add, [p[1:2] * jnp.exp(p[0:1] - best) for p in pairs])
        return stacked(best, mass)

    t1_out[...] = stacked(as_row(top[:, 0:1]), as_row(total))
    copies = stage_x(t1_out, t1_in, t1_send, t1_recv)
    start(copies)
    arrived(copies)
    t2_out[...] = joined([t1_out[...]] + [t1_in[i] for i in range(7)])
    copies = stage_z(t2_out, t2_in, t2_send, t2_recv)
    start(copies)
    arrived(copies)
    t3_out[...] = joined([t2_out[...]] + [t2_in[i] for i in range(3)])
    t3_copies = stage_y(t3_out, t3_in, t3_send, t3_recv)
    start(t3_copies)
    load_weight.wait()

    def contribute(g):
        stats = t3_out[...] if g == 0 else t3_in[g - 1]
        best = as_column(stats[0:1])
        inverse = as_column(1.0 / stats[1:2])

        def normalise(j, carry):
            part = raw[g, :, pl.ds(pl.multiple_of(j * BLK, BLK), BLK)].astype(F32)
            prob[j] = (jnp.exp(part - best) * inverse).astype(BF16)
            return carry

        lax.fori_loop(0, OLD, normalise, 0, unroll=2)

        def slot(o, acc):
            for k in range(2):
                e = entry_ref[o * 2 + k]
                product = jnp.dot(prob[e // FAN], weight[e], preferred_element_type=F32)
                product = product.astype(BF16)
                out1[g, o // (NZ * NC), (o // NC) % NZ, o % NC, k] = product
                acc = acc + product.astype(F32) * valid_ref[o * 2 + k]
            return acc

        acc = lax.fori_loop(0, 32, slot, jnp.zeros((ROWS, BLK), F32), unroll=2)
        mass_acc[g] = acc
        start([first_copy(g, h, i) for i in range(7) for h in (0, 1)])

    def merge(g, h):
        arrived([first_copy(g, h, i) for i in range(7)])

        def piece(t, carry):
            q, rows = t // 2, pl.ds(pl.multiple_of((t % 2) * 32, 32), 32)
            own = pl.ds(pl.multiple_of(h * HALF + (t % 2) * 32, 32), 32)
            sums = [jnp.zeros((32, BLK), F32) for _ in range(PER)]
            for i in range(8):
                for k in range(2):
                    if i < 7:
                        part, hit = in1[g, h, i, q, k, rows], masks[h, i, q, k]
                    elif h == 0:
                        part, hit = out1[g, x, q, c, k, own], mask_ref[x, q, c, k]
                    else:
                        part, hit = out1[g, q, z, c, k, own], mask_ref[q, z, c, k]
                    part = part.astype(F32)
                    for b in range(PER):
                        sums[b] = sums[b] + part * hit[b : b + 1]
            for b in range(PER):
                out2[g, h, q, b, rows] = sums[b].astype(BF16)
            return carry

        lax.fori_loop(0, 8, piece, 0)
        start([second_copy(g, h, d) for d in (1, 2, 3)])

    contribute(0)
    arrived([raw_copies[0]])
    start([raw_copies[2]])
    arrived([raw_copies[1]])
    start([raw_copies[3]])
    arrived(t3_copies)
    contribute(1)
    load_hidden.wait()
    contribute(3)
    arrived(mask_copies)
    hidden_copies = [hidden_copy(d) for d in (1, 2, 3)]
    merge(0, 0)
    merge(0, 1)
    arrived(raw_copies[2:])
    start(hidden_copies)
    contribute(2)
    merge(1, 0)
    merge(1, 1)
    merge(3, 0)
    merge(3, 1)
    arrived(hidden_copies)
    sibling_copies = [sibling_copy(d) for d in (1, 2, 3)]
    start(sibling_copies)
    merge(2, 0)
    merge(2, 1)
    arrived(sibling_copies)
    keep = pltpu.make_async_copy(hidden, everyone_hbm, local_sem.at[4])
    keep.start()
    load_head.wait()

    def columns_of(n, carry):
        columns = pl.ds(pl.multiple_of(n * 256, 256), 256)
        logits[:, columns] = jnp.dot(hidden[...], head[:, columns], preferred_element_type=F32)
        return carry

    lax.fori_loop(0, VN // 256, columns_of, 0)

    sublane3 = lax.broadcasted_iota(jnp.int32, (8, BLK), 0)

    def triple(first, second, third):
        wide = [jnp.broadcast_to(r, (8, BLK)) for r in (first, second, third)]
        return jnp.where(sublane3 == 0, wide[0], jnp.where(sublane3 == 1, wide[1], wide[2]))

    for g in range(NY):
        group = (y - g + NY) % NY
        rows = pl.ds(pl.multiple_of(group * ROWS, ROWS), ROWS)
        best = logits[rows, pl.ds(0, BLK)]
        for b in range(1, PER):
            best = jnp.maximum(best, logits[rows, pl.ds(b * BLK, BLK)])
        best = jnp.broadcast_to(jnp.max(best, axis=1, keepdims=True), (ROWS, BLK))
        acc = jnp.zeros((ROWS, BLK), F32)
        for b in range(PER):
            acc = acc + jnp.exp(logits[rows, pl.ds(b * BLK, BLK)] - best)
        a1_out[group] = triple(
            as_row(best[:, 0:1]),
            as_row(jnp.sum(acc, axis=1, keepdims=True)),
            as_row(jnp.sum(mass_acc[g], axis=1, keepdims=True)),
        )

    def joined3(parts):
        best = functools.reduce(jnp.maximum, [p[0:1] for p in parts])
        exps = functools.reduce(jnp.add, [p[1:2] * jnp.exp(p[0:1] - best) for p in parts])
        mass = functools.reduce(jnp.add, [p[2:3] for p in parts])
        return triple(best, exps, mass)

    def combine(out, own, into, count):
        for q in range(NY):
            out[q] = joined3([own[q]] + [into[i, q] for i in range(count)])

    copies = stage_x(a1_out, a1_in, a1_send, a1_recv)
    start(copies)
    arrived(copies)
    combine(a2_out, a1_out, a1_in, 7)
    copies = stage_z(a2_out, a2_in, a2_send, a2_recv)
    start(copies)
    arrived(copies)
    combine(a3_out, a2_out, a2_in, 3)
    copies = stage_y(a3_out, a3_in, a3_send, a3_recv)
    start(copies)
    arrived(copies)
    for q in range(NY):
        stats = joined3([a3_out[q]] + [a3_in[i, q] for i in range(3)])
        rows = pl.ds(q * ROWS, ROWS)
        log_total[rows] = as_column(stats[0:1] + jnp.log(stats[1:2]))
        mass_plus[rows] = as_column(stats[2:3] + 1.0)
        f1_out[q] = stats

    mine = f1_out[y]
    own_log = mine[0:1] + jnp.log(mine[1:2])
    own_terms = mine[2:3] * own_log + own_log

    base = (y * (NX * NZ * NC) + v) * VN
    lane = lax.broadcasted_iota(jnp.int32, (32, BLK), 1) + base

    def finish(g, h):
        arrived([second_copy(g, h, d) for d in (1, 2, 3)])
        group = (y - g + NY) % NY
        q = z if h == 0 else x

        def piece(t, carry):
            part = pl.ds(pl.multiple_of(t * 32, 32), 32)
            rows = pl.ds(pl.multiple_of(group * ROWS + h * HALF + t * 32, 32), 32)
            log_here, mass_here, label_here = log_total[rows], mass_plus[rows], label_ref[rows]
            acc = jnp.zeros((32, BLK), F32)
            for b in range(PER):
                target = out2[g, h, q, b, part].astype(F32)
                for d in range(3):
                    target = target + in2[g, h, d, b, part].astype(F32)
                columns = pl.ds(b * BLK, BLK)
                here = logits[rows, columns]
                hit = (label_here == lane + b * BLK).astype(F32)
                acc = acc + (target + hit) * here
                grad = mass_here * jnp.exp(here - log_here) - target - hit
                grad_ref[rows, columns] = grad.astype(BF16)
            rest[rows] = acc
            return carry

        lax.fori_loop(0, HALF // 32, piece, 0)

    for g in (0, 1, 3, 2):
        for h in (0, 1):
            finish(g, h)

    for q in range(NY):
        column = jnp.sum(rest[pl.ds(q * ROWS, ROWS)], axis=1, keepdims=True)
        f1_out[q] = jnp.broadcast_to(as_row(column), (8, BLK))
    copies = [remote(f1_out.at[(y + d) % NY], f1_in.at[d - 1], f1_send.at[d - 1],
                     f1_recv.at[d - 1], along_y(d)) for d in (1, 2, 3)]
    start(copies)
    arrived(copies)
    f2_out[...] = f1_out[y] + (f1_in[0] + f1_in[1] + f1_in[2])
    copies = stage_x(f2_out, f2_in, f2_send, f2_recv)
    start(copies)
    arrived(copies)
    f3_out[...] = functools.reduce(jnp.add, [f2_out[...]] + [f2_in[i] for i in range(7)])
    copies = stage_z(f3_out, f3_in, f3_send, f3_recv)
    start(copies)
    arrived(copies)
    everything = f3_out[...] + (f3_in[0] + f3_in[1] + f3_in[2])
    loss_ref[...] = own_terms - everything[0:1]

    keep.wait()
    for copy in pending:
        copy.wait_send()


def exchange(entry, valid, mask, label, raw, hidden, head, weight):
    dma = pltpu.SemaphoreType.DMA
    vmem = pltpu.VMEM
    tile, quad = (8, BLK), (NY, 8, BLK)
    scratch = [
        vmem((NY, ROWS, OLD * BLK), BF16),
        vmem((OLD, ROWS, BLK), BF16),
        vmem((ENT, BLK, BLK), BF16),
        vmem((NY * ROWS, D), BF16),
        vmem((D, VN), BF16),
        vmem((NY * ROWS, VN), F32),
        vmem((NY, NX, NZ, NC, 2, ROWS, BLK), BF16),
        vmem((NY, 2, 7, 4, 2, HALF, BLK), BF16),
        vmem((NY, 2, 4, PER, HALF, BLK), BF16),
        vmem((NY, 2, 3, PER, HALF, BLK), BF16),
        vmem((2, 7, 4, 2, 8, BLK), F32),
        vmem((NY, ROWS, BLK), F32),
        vmem((NY * ROWS, BLK), F32),
        vmem((NY * ROWS, BLK), F32),
        vmem((NY * ROWS, BLK), F32),
        vmem(tile, F32), vmem((7,) + tile, F32),
        vmem(tile, F32), vmem((3,) + tile, F32),
        vmem(tile, F32), vmem((3,) + tile, F32),
        vmem(quad, F32), vmem((7,) + quad, F32),
        vmem(quad, F32), vmem((3,) + quad, F32),
        vmem(quad, F32), vmem((3,) + quad, F32),
        vmem(quad, F32), vmem((3,) + tile, F32),
        vmem(tile, F32), vmem((7,) + tile, F32),
        vmem(tile, F32), vmem((3,) + tile, F32),
        dma((5,)), dma((4,)), dma((4,)), dma((2, 7)), dma((2, 7)),
        dma((NY, 2, 7)), dma((NY, 2, 7)), dma((NY, 2, 3)), dma((NY, 2, 3)),
        dma((3,)), dma((3,)), dma((3,)), dma((3,)),
    ]
    for count in (7, 3, 3, 7, 3, 3, 3, 7, 3):
        scratch += [dma((count,)), dma((count,))]
    smem = pl.BlockSpec(memory_space=pltpu.SMEM)
    inside = pl.BlockSpec(memory_space=pltpu.VMEM)
    outside = pl.BlockSpec(memory_space=pl.ANY)
    return pl.pallas_call(
        exchange_kernel,
        out_shape=(
            jax.ShapeDtypeStruct((1, ROWS), F32),
            jax.ShapeDtypeStruct((NY * ROWS, VN), BF16),
            jax.ShapeDtypeStruct((NY * ROWS, D), BF16),
        ),
        in_specs=[smem, smem, inside, inside] + [outside] * 4,
        out_specs=(inside, inside, outside),
        scratch_shapes=scratch,
        compiler_params=pltpu.CompilerParams(
            collective_id=0, has_side_effects=True, vmem_limit_bytes=60 << 20
        ),
        name="exchange",
    )(entry, valid, mask, label, raw, hidden, head, weight)


GRAD_ROWS = 512


def grad_kernel(hidden_ref, grad_ref, out_ref):
    out_ref[...] = lax.dot_general(
        hidden_ref[...], grad_ref[...], (((0,), (0,)), ((), ())), preferred_element_type=F32
    ).astype(BF16)


def head_gradient(hidden, grad):
    return pl.pallas_call(
        grad_kernel,
        grid=(D // GRAD_ROWS,),
        out_shape=jax.ShapeDtypeStruct((D, VN), BF16),
        in_specs=[
            pl.BlockSpec((NY * ROWS, GRAD_ROWS), lambda i: (0, i)),
            pl.BlockSpec((NY * ROWS, VN), lambda i: (0, 0)),
        ],
        out_specs=pl.BlockSpec((GRAD_ROWS, VN), lambda i: (i, 0)),
        compiler_params=pltpu.CompilerParams(vmem_limit_bytes=32 << 20),
        name="head_gradient",
    )(hidden, grad)


def local(teacher_logits, hidden, new_head, labels, map_target, map_weight):
    y = lax.axis_index("tok")
    nodes = NX * NZ * NC
    flat = map_target.reshape(1, ENT)
    owner = flat // PER - y * nodes
    match = owner == jnp.arange(nodes, dtype=jnp.int32)[:, None]
    index = jnp.arange(ENT, dtype=jnp.int32)[None, :]
    key = index * PER + flat % PER
    none = ENT * PER
    first = jnp.min(jnp.where(match, key, none), axis=1)
    last = jnp.max(jnp.where(match, key, -1), axis=1)
    keys = jnp.stack([first, last], axis=1)
    valid = jnp.stack([first < none, last > first], axis=1)
    keys = jnp.where(valid, keys, 0)
    entry = (keys // PER).reshape(2 * nodes)
    block = (keys % PER)[:, :, None]
    mask = (block == jnp.arange(PER)[None, None, :]) & valid[:, :, None]
    mask = jnp.broadcast_to(mask.astype(F32)[..., None], (nodes, 2, PER, BLK))
    mask = mask.reshape(NX, NZ, NC, 2, PER, BLK)
    label = jnp.broadcast_to(labels[:, None], (NY * ROWS, BLK))
    loss, grad, everyone = exchange(
        entry, valid.astype(F32).reshape(2 * nodes), mask, label,
        teacher_logits, hidden, new_head, map_weight.reshape(ENT, BLK, BLK),
    )
    return loss.reshape(ROWS), head_gradient(everyone, grad)


def solution(mesh):
    return jax.shard_map(
        local,
        mesh=mesh,
        in_specs=(
            P("tok", "vocab"),
            P("tok", None),
            P(None, ("tok", "vocab")),
            P(),
            P("vocab", None),
            P("vocab", None, None, None),
        ),
        out_specs=(P("tok"), P(None, ("tok", "vocab"))),
        check_vma=False,
    )
```

time: 479 us -> 139 us (0.29)
  blocking collectives: 377 us -> 0 us
  Pallas kernels: 0 us -> 128 us
  matrix products: 33.3 us -> 0 us
  local copies, waits for them, and re-layouts: 41.4 us -> 8.88 us
  between operations: 14.2 us -> 0.73 us
  starting transfers between devices: 5.46 us -> 0 us
  other arithmetic: 5.87 us -> 0.87 us
    psum x2 -> x0, blocking collectives: 130 us -> none  [the longest x1 67 us: local(): lax.psum(jnp.sum(jnp.exp(scores - highest[:, None]), axis=1), 'vocab')]
    pmax x2 -> x0, blocking collectives: 130 us -> none  [the longest x1 65 us: local(): top_all = lax.pmax(row_top, ('tok', 'vocab'))]
    pallas_call x0 -> x2, Pallas kernels: none -> 128 us  [the longest x1 120 us: exchange(): pl.pallas_call(exchange_kernel, out_shape=(jax.ShapeDtypeStruct((1, ROWS)...]
    all_gather x1 -> x0, blocking collectives: 117 us -> none  [local(): lax.all_gather(map_target, 'vocab', axis=0, tiled=True)]
    dot_general x5 -> x0, matrix products: 33.3 us -> none  [the longest x1 10.9 us: local(): lax.dot_general(everyone, grad_logits, (((0,), (0,)), ((), ())), preferre...]
    scatter x1 -> x0, local copies, waits for them, and re-layouts: 20.7 us -> none  [local(): jnp.zeros((nodes, capacity, tok_rows, block), jnp.bfloat16)]
    unnamed x12 -> x8, local copies, waits for them, and re-layouts: 14.1 us -> 4.83 us
    all_to_all x1 -> x0, starting transfers between devices: 5.43 us -> none  [local(): lax.all_to_all(outbox, ('tok', 'vocab'), split_axis=0, concat_axis=0, til...]
  transfers between devices with their start and end apart: 2 -> 0, of which waited for: 0 -> 0; matrix products, arithmetic and copies ran while one was open for 9% -> 0% of each run, Pallas kernels for 0% -> 0%
where the time goes in v1:
time: 139 us
  Pallas kernels  128 us (92%)
  local copies, waits for them, and re-layouts  8.88 us (6%)
    pallas_call x1, Pallas kernels, exchange(): pl.pallas_call(exchange_kernel, out_shape=(jax.ShapeDtypeStruct((1, ROWS)...  120 us
    pallas_call x1, Pallas kernels, head_gradient(): pl.pallas_call(grad_kernel, grid=(D // GRAD_ROWS,), out_shape=jax.ShapeDt...  8.74 us
    unnamed x8, local copies, waits for them, and re-layouts  4.83 us

profile of v1, /device:TPU:1, one launch (start us, length us, event | category | flops | bytes accessed | tf_op | source)
XLA Modules:
  0.0 139.0 jit_solution(14392341624139561747)
XLA Ops:
  0.6 0.8 copy.18
  1.4 0.1 reshape.214
  1.5 0.1 select_reduce_fusion.1
  1.7 0.1 reduce_min.15
  1.8 0.1 reduce_max.15
  2.0 0.2 copy.21
  2.2 0.2 copy.22
  2.4 0.1 and_convert_fusion
  2.5 0.1 copy.19
  2.6 0.1 select_n.66
  2.7 0.5 and_select_fusion.entry_ref
  3.2 0.1 copy.20
  3.3 0.7 reshape.217.valid_ref
  4.0 0.8 broadcast_in_dim.49.mask_ref
  4.9 1.5 %broadcast_in_dim.50.label_ref = s32[512,128]{1,0:T(8,128)} broadcast(s32[512]{0:T(512)} %param.9), dimensions={0} | broadcast | bytes 264192 | tf_op jit(solution)/shard_map/broadcast_in_dim | solution.py:510
  6.4 119.7 %exchange.1 = (f32[1,128]{1,0:T(1,128)}, bf16[512,1024]{1,0:T(8,128)(2,1)}, bf16[512,4608]{1,0:T(8,128)(2,1)}) custom-call(s32[64]{0:T(128)} %and_select_fusion.entry_ref, f32[64]{0:T(128)} %reshape.217.valid_ref, f32[4,4,2,2,8,128]{5,4,3,2,1,0:T(8,128)} %broadcast_in_dim.49.mask_ref, s32[512,128]{1,0:T(8,128)} %broadcast_in_dim.50.label_ref, ...), custom_call_target="tpu_custom_call" | custom-call | tf_op jit(solution)/shard_map/exchange/pallas_call | solution.py:450
  126.1 0.0 copy-start
  126.1 2.3 %copy-done = bf16[512,4608]{1,0:T(8,128)(2,1)S(1)} copy-done((bf16[512,4608]{1,0:T(8,128)(2,1)S(1)}, bf16[512,4608]{1,0:T(8,128)(2,1)}, u32[]{:S(2)}) %copy-start) | copy-done | bytes 4718616
  128.5 0.0 copy-start.1
  128.5 1.2 copy-done.1
  129.7 0.0 copy-start.2
  129.7 8.7 %head_gradient.1 = bf16[4608,1024]{1,0:T(8,128)(2,1)} custom-call(bf16[512,4608]{1,0:T(8,128)(2,1)S(1)} %copy-done, bf16[512,1024]{1,0:T(8,128)(2,1)S(1)} %copy-done.1), custom_call_target="tpu_custom_call" | custom-call | tf_op jit(solution)/shard_map/head_gradient/pallas_call | solution.py:477
  138.4 0.0 copy-done.2
  138.4 0.5 copy.24
  (7 shorter events, 0.1 us)
Async XLA Ops:
  126.1 2.3 %copy-start = (bf16[512,4608]{1,0:T(8,128)(2,1)S(1)}, bf16[512,4608]{1,0:T(8,128)(2,1)}, u32[]{:S(2)}) copy-start(bf16[512,4608]{1,0:T(8,128)(2,1)} %get-tuple-element.6.hidden_ref) | copy-start | bytes 14155780
  128.5 1.2 copy-start.1
  129.7 8.7 %copy-start.2 = (f32[1,128]{1,0:T(1,128)S(1)}, f32[1,128]{1,0:T(1,128)}, u32[]{:S(2)}) copy-start(f32[1,128]{1,0:T(1,128)} %get-tuple-element.5) | copy-start | bytes 1540

commit v2 on v1

v2 whole, which is shorter than its diff:
```python
import functools

import jax
import jax.numpy as jnp
from jax import lax
from jax.experimental import pallas as pl
from jax.experimental.pallas import tpu as pltpu
from jax.sharding import PartitionSpec as P

MESH = pl.DeviceIdType.MESH
F32 = jnp.float32
BF16 = jnp.bfloat16

NY = 4
NX = 4
NZ = 4
NC = 2
ROWS = 128
CHUNK = 64
HALF = CHUNK // 2
NU = NY * ROWS // CHUNK
BLK = 128
FAN = 4
D = 4608
HD = D // 2
VN = 1024
PER = 8
OLD = 32
ENT = OLD * FAN

FIRST = [(0, 1), (1, 0), (1, 1), (2, 0), (2, 1), (3, 0), (3, 1)]


def vocab_index(x, z, c):
    return (x * NZ + z) * NC + c


def as_row(column):
    return jnp.transpose(jnp.broadcast_to(column, (ROWS, BLK)))[0:1, :]


def as_column(row):
    return jnp.transpose(jnp.broadcast_to(row, (ROWS, BLK)))


def exchange_kernel(
    key_ref, label_ref, raw_hbm, hidden_hbm, head_hbm, weight_hbm,
    loss_ref, grad_ref, everyone_hbm,
    mask_ref, raw, prob, weight, hidden, head, logits, target, out1, in1, out2, in2, masks, mass_acc,
    log_total, mass_plus, label_at, rest,
    t1_out, t1_in, t2_out, t2_in, t3_out, t3_in,
    a1_out, a1_in, a2_out, a2_in, a3_out, a3_in,
    f1_out, f1_in, f2_out, f2_in, f3_out, f3_in,
    local_sem, raw_send, raw_recv, mask_send, mask_recv, p1_send, p1_recv, p2_send, p2_recv,
    hid_send, hid_recv, sib_send, sib_recv,
    t1_send, t1_recv, t2_send, t2_recv, t3_send, t3_recv,
    a1_send, a1_recv, a2_send, a2_recv, a3_send, a3_recv,
    f1_send, f1_recv, f2_send, f2_recv, f3_send, f3_recv,
):
    y = lax.axis_index("tok")
    v = lax.axis_index("vocab")
    x = v // (NZ * NC)
    z = (v // NC) % NZ
    c = v % NC

    def remote(src, dst, send, recv, device):
        return pltpu.make_async_remote_copy(
            src_ref=src, dst_ref=dst, send_sem=send, recv_sem=recv,
            device_id=device, device_id_type=MESH,
        )

    def along_x(step, core_step=0):
        return (y, vocab_index((x + step) % NX, z, (c + core_step) % NC))

    def along_z(step, core_step=0):
        return (y, vocab_index(x, (z + step) % NZ, (c + core_step) % NC))

    def along_y(step):
        return ((y + step) % NY, v)

    load_raw = pltpu.make_async_copy(raw_hbm, raw.at[0], local_sem.at[0])
    load_weight = pltpu.make_async_copy(weight_hbm, weight, local_sem.at[1])
    own_rows = pl.ds(pl.multiple_of(y * ROWS, ROWS), ROWS)
    load_hidden = pltpu.make_async_copy(hidden_hbm, hidden.at[own_rows], local_sem.at[2])
    load_head = pltpu.make_async_copy(head_hbm, head, local_sem.at[3])
    load_raw.start()

    barrier = pltpu.get_barrier_semaphore()
    partners = [along_x(da, dc) for da, dc in FIRST]
    partners += [along_z(da, dc) for da, dc in FIRST if da]
    partners += [along_y(step) for step in (1, 2, 3)]
    for partner in partners:
        pl.semaphore_signal(barrier, inc=1, device_id=partner, device_id_type=MESH)
    pl.semaphore_wait(barrier, len(partners))

    def first_partner(h, i):
        da, dc = FIRST[i]
        return along_x(da, dc) if h == 0 else along_z(da, dc)

    def mask_copy(h, i):
        da, dc = FIRST[i]
        c2 = (c + dc) % NC
        if h == 0:
            src = mask_ref.at[(x + da) % NX, :, c2]
        else:
            src = mask_ref.at[:, (z + da) % NZ, c2]
        return remote(src, masks.at[h, i], mask_send.at[h, i], mask_recv.at[h, i],
                      first_partner(h, i))

    def first_copy(u, h, i):
        da, dc = FIRST[i]
        c2 = (c + dc) % NC
        rows = pl.ds(h * HALF, HALF)
        if h == 0:
            src = out1.at[u, (x + da) % NX, :, c2, :, rows]
        else:
            src = out1.at[u, :, (z + da) % NZ, c2, :, rows]
        return remote(src, in1.at[u, h, i], p1_send.at[u, h, i], p1_recv.at[u, h, i],
                      first_partner(h, i))

    def second_copy(u, h, d):
        if h == 0:
            q, device = (z + d) % NZ, along_z(d)
        else:
            q, device = (x + d) % NX, along_x(d)
        return remote(out2.at[u, h, q], in2.at[u, h, d - 1], p2_send.at[u, h, d - 1],
                      p2_recv.at[u, h, d - 1], device)

    upper, lower = pl.ds(0, CHUNK), pl.ds(CHUNK, CHUNK)
    raw_copies = [
        remote(raw.at[source, rows], raw.at[into, rows], raw_send.at[i], raw_recv.at[i], along_y(d))
        for i, (source, into, rows, d) in enumerate([
            (0, 1, upper, 1), (0, 3, lower, 3), (0, 1, lower, 1), (0, 3, upper, 3),
            (1, 2, upper, 1), (3, 2, lower, 3),
        ])
    ]

    own_columns = pl.ds(pl.multiple_of(c * HD, HD), HD)

    def hidden_part(d, first=0, count=ROWS):
        start_row = ((y - d + NY) % NY) * ROWS + first
        rows = pl.ds(pl.multiple_of(start_row, CHUNK), count)
        return hidden.at[rows, own_columns]

    hidden_copies = [
        remote(hidden_part(*what), hidden_part(*what), hid_send.at[i], hid_recv.at[i], along_y(d))
        for i, (what, d) in enumerate([
            ((0, 0, CHUNK), 1), ((0, CHUNK, CHUNK), 3), ((0, CHUNK, CHUNK), 1), ((0, 0, CHUNK), 3),
            ((1, 0, CHUNK), 1), ((3, CHUNK, CHUNK), 3),
        ])
    ]

    def sibling_copy(d):
        part = hidden_part(d)
        return remote(part, part, sib_send.at[d - 1], sib_recv.at[d - 1], along_x(0, 1))

    def stage_x(out, into, send, recv):
        return [remote(out, into.at[i], send.at[i], recv.at[i], first_partner(0, i))
                for i in range(7)]

    def stage_z(out, into, send, recv):
        return [remote(out, into.at[d - 1], send.at[d - 1], recv.at[d - 1], along_z(d))
                for d in (1, 2, 3)]

    def stage_y(out, into, send, recv):
        return [remote(out, into.at[d - 1], send.at[d - 1], recv.at[d - 1], along_y(d))
                for d in (1, 2, 3)]

    pending = []

    def start(copies):
        for copy in copies:
            copy.start()
        pending.extend(copies)

    def arrived(copies):
        for copy in copies:
            copy.wait_recv()

    sublane = lax.broadcasted_iota(jnp.int32, (8, BLK), 0)

    def mask_rows(o, carry):
        for k in range(2):
            key = key_ref[o * 2 + k]
            row = jnp.where(key < 0, -1, key % PER)
            mask_ref[o // (NZ * NC), (o // NC) % NZ, o % NC, k] = (sublane == row).astype(F32)
        return carry

    lax.fori_loop(0, NX * NZ * NC, mask_rows, 0, unroll=4)
    load_raw.wait()
    start(raw_copies[:2])
    load_weight.start()
    load_hidden.start()
    load_head.start()
    mask_copies = [mask_copy(h, i) for h in (0, 1) for i in range(7)]
    start(mask_copies)

    def block_max(j, acc):
        part = raw[0, :, pl.ds(pl.multiple_of(j * BLK, BLK), BLK)].astype(F32)
        return jnp.maximum(acc, part)

    top = lax.fori_loop(1, OLD, block_max, raw[0, :, pl.ds(0, BLK)].astype(F32), unroll=4)
    top = jnp.broadcast_to(jnp.max(top, axis=1, keepdims=True), (ROWS, BLK))

    def block_sum(j, acc):
        part = raw[0, :, pl.ds(pl.multiple_of(j * BLK, BLK), BLK)].astype(F32)
        return acc + jnp.exp(part - top)

    total = lax.fori_loop(0, OLD, block_sum, jnp.zeros((ROWS, BLK), F32), unroll=4)
    total = jnp.sum(total, axis=1, keepdims=True)
    def stacked(first, second):
        return jnp.where(sublane == 0, jnp.broadcast_to(first, (8, BLK)),
                         jnp.broadcast_to(second, (8, BLK)))

    def joined(pairs):
        best = functools.reduce(jnp.maximum, [p[0:1] for p in pairs])
        mass = functools.reduce(jnp.add, [p[1:2] * jnp.exp(p[0:1] - best) for p in pairs])
        return stacked(best, mass)

    t1_out[...] = stacked(as_row(top[:, 0:1]), as_row(total))
    copies = stage_x(t1_out, t1_in, t1_send, t1_recv)
    start(copies)
    arrived(copies)
    t2_out[...] = joined([t1_out[...]] + [t1_in[i] for i in range(7)])
    copies = stage_z(t2_out, t2_in, t2_send, t2_recv)
    start(copies)
    arrived(copies)
    t3_out[...] = joined([t2_out[...]] + [t2_in[i] for i in range(3)])
    t3_copies = stage_y(t3_out, t3_in, t3_send, t3_recv)
    start(t3_copies)
    load_weight.wait()

    def contribute(g, part):
        u = g * 2 + part
        tokens = pl.ds(part * CHUNK, CHUNK)
        stats = t3_out[...] if g == 0 else t3_in[g - 1]
        best = as_column(stats[0:1])[part * CHUNK : (part + 1) * CHUNK]
        inverse = as_column(1.0 / stats[1:2])[part * CHUNK : (part + 1) * CHUNK]

        def normalise(j, carry):
            scores = raw[g, tokens, pl.ds(pl.multiple_of(j * BLK, BLK), BLK)].astype(F32)
            prob[j] = (jnp.exp(scores - best) * inverse).astype(BF16)
            return carry

        lax.fori_loop(0, OLD, normalise, 0, unroll=4)

        def slot(o, acc):
            for k in range(2):
                key = key_ref[o * 2 + k]
                e = jnp.maximum(key, 0) // PER
                filled = jnp.where(key < 0, 0.0, 1.0)
                product = jnp.dot(prob[e // FAN], weight[e], preferred_element_type=F32)
                product = product.astype(BF16)
                out1[u, o // (NZ * NC), (o // NC) % NZ, o % NC, k] = product
                acc = acc + product.astype(F32) * filled
            return acc

        acc = lax.fori_loop(0, 32, slot, jnp.zeros((CHUNK, BLK), F32), unroll=4)
        mass_acc[g, tokens] = acc
        start([first_copy(u, h, i) for i in range(7) for h in (0, 1)])

    def merge(u, h):
        arrived([first_copy(u, h, i) for i in range(7)])
        own = pl.ds(h * HALF, HALF)

        def piece(q, carry):
            sums = [jnp.zeros((HALF, BLK), F32) for _ in range(PER)]
            for i in range(8):
                for k in range(2):
                    if i < 7:
                        part, hit = in1[u, h, i, q, k], masks[h, i, q, k]
                    elif h == 0:
                        part, hit = out1[u, x, q, c, k, own], mask_ref[x, q, c, k]
                    else:
                        part, hit = out1[u, q, z, c, k, own], mask_ref[q, z, c, k]
                    part = part.astype(F32)
                    for b in range(PER):
                        sums[b] = sums[b] + part * hit[b : b + 1]
            for b in range(PER):
                out2[u, h, q, b] = sums[b].astype(BF16)
            return carry

        lax.fori_loop(0, 4, piece, 0)
        start([second_copy(u, h, d) for d in (1, 2, 3)])

    def merge_all(*units):
        for u in units:
            for h in (0, 1):
                merge(u, h)

    def group_rows(g, first=0, count=ROWS):
        start_row = ((y - g + NY) % NY) * ROWS + first
        return pl.ds(pl.multiple_of(start_row, HALF), count)

    def student(g):
        rows = group_rows(g)

        def columns_of(n, carry):
            columns = pl.ds(pl.multiple_of(n * 256, 256), 256)
            logits[rows, columns] = jnp.dot(
                hidden[rows, :], head[:, columns], preferred_element_type=F32
            )
            return carry

        lax.fori_loop(0, VN // 256, columns_of, 0)
        best = logits[rows, pl.ds(0, BLK)]
        for b in range(1, PER):
            best = jnp.maximum(best, logits[rows, pl.ds(b * BLK, BLK)])
        best = jnp.broadcast_to(jnp.max(best, axis=1, keepdims=True), (ROWS, BLK))
        acc = jnp.zeros((ROWS, BLK), F32)
        for b in range(PER):
            acc = acc + jnp.exp(logits[rows, pl.ds(b * BLK, BLK)] - best)
        a1_out[(y - g + NY) % NY] = triple(
            as_row(best[:, 0:1]),
            as_row(jnp.sum(acc, axis=1, keepdims=True)),
            as_row(jnp.sum(mass_acc[g], axis=1, keepdims=True)),
        )

    def triple(first, second, third):
        wide = [jnp.broadcast_to(r, (8, BLK)) for r in (first, second, third)]
        return jnp.where(sublane == 0, wide[0], jnp.where(sublane == 1, wide[1], wide[2]))

    base = (y * (NX * NZ * NC) + v) * VN
    lane = (lax.broadcasted_iota(jnp.int32, (HALF, BLK), 1) + base).astype(F32)
    for q in range(NY):
        label_at[pl.ds(q * ROWS, ROWS)] = as_column(label_ref[pl.ds(q, 1)].astype(F32))

    def settle(u, h):
        arrived([second_copy(u, h, d) for d in (1, 2, 3)])
        q = z if h == 0 else x
        rows = group_rows(u // 2, (u % 2) * CHUNK + h * HALF, HALF)
        label_here = label_at[rows]
        acc = jnp.zeros((HALF, BLK), F32)
        for b in range(PER):
            here = out2[u, h, q, b].astype(F32)
            for d in range(3):
                here = here + in2[u, h, d, b].astype(F32)
            columns = pl.ds(b * BLK, BLK)
            hit = (label_here == lane + float(b * BLK)).astype(F32)
            here = here + hit
            target[rows, columns] = here
            acc = acc + here * logits[rows, columns]
        rest[rows] = acc

    def settle_all(*units):
        for u in units:
            for h in (0, 1):
                settle(u, h)

    def gradients(first, count):
        def piece(t, carry):
            rows = pl.ds(pl.multiple_of(t * 32, 32), 32)
            log_here, mass_here = log_total[rows], mass_plus[rows]
            for b in range(PER):
                columns = pl.ds(b * BLK, BLK)
                grad = mass_here * jnp.exp(logits[rows, columns] - log_here) - target[rows, columns]
                grad_ref[rows, columns] = grad.astype(BF16)
            return carry

        lax.fori_loop(first, first + count, piece, 0)

    def joined3(parts):
        best = functools.reduce(jnp.maximum, [p[0:1] for p in parts])
        exps = functools.reduce(jnp.add, [p[1:2] * jnp.exp(p[0:1] - best) for p in parts])
        mass = functools.reduce(jnp.add, [p[2:3] for p in parts])
        return triple(best, exps, mass)

    def combine(out, own, into, count):
        for q in range(NY):
            out[q] = joined3([own[q]] + [into[i, q] for i in range(count)])

    def loss_part(g):
        column = jnp.sum(rest[group_rows(g)], axis=1, keepdims=True)
        f1_out[g] = jnp.broadcast_to(as_row(column), (8, BLK))

    def loss_copy(g):
        return remote(f1_out.at[g], f1_in.at[g - 1], f1_send.at[g - 1], f1_recv.at[g - 1],
                      along_y(NY - g))

    contribute(0, 0)
    contribute(0, 1)
    arrived(raw_copies[0:2])
    start(raw_copies[2:4])
    arrived(t3_copies)
    contribute(1, 0)
    contribute(3, 1)
    arrived(mask_copies)
    merge_all(0, 1)
    arrived(raw_copies[2:4])
    start(raw_copies[4:6])
    contribute(1, 1)
    contribute(3, 0)
    load_hidden.wait()
    load_head.wait()
    merge_all(2, 7)
    arrived(raw_copies[4:6])
    start(hidden_copies[0:4])
    contribute(2, 0)
    contribute(2, 1)
    student(0)
    merge_all(3, 6)
    arrived(hidden_copies[0:4])
    start(hidden_copies[4:6])
    sibling_copies = [sibling_copy(d) for d in (1, 3, 2)]
    start(sibling_copies[:2])
    arrived(sibling_copies[:2])
    student(1)
    student(3)
    arrived(hidden_copies[4:6])
    start(sibling_copies[2:])
    arrived(sibling_copies[2:])
    student(2)
    keep = pltpu.make_async_copy(hidden, everyone_hbm, local_sem.at[4])
    keep.start()

    copies = stage_y(a1_out, a1_in, a1_send, a1_recv)
    start(copies)
    settle_all(0, 1)
    arrived(copies)
    combine(a2_out, a1_out, a1_in, 3)
    copies = stage_x(a2_out, a2_in, a2_send, a2_recv)
    start(copies)
    merge_all(4)
    arrived(copies)
    combine(a3_out, a2_out, a2_in, 7)
    copies = stage_z(a3_out, a3_in, a3_send, a3_recv)
    start(copies)
    merge_all(5)
    settle_all(2, 7)
    arrived(copies)
    for q in range(NY):
        stats = joined3([a3_out[q]] + [a3_in[i, q] for i in range(3)])
        rows = pl.ds(q * ROWS, ROWS)
        log_total[rows] = as_column(stats[0:1] + jnp.log(stats[1:2]))
        mass_plus[rows] = as_column(stats[2:3] + 1.0)
        f1_out[q] = stats

    mine = f1_out[y]
    own_log = mine[0:1] + jnp.log(mine[1:2])
    own_terms = mine[2:3] * own_log + own_log
    settle_all(3, 6)
    for g in (0, 1, 3):
        loss_part(g)
    loss_copies = [loss_copy(g) for g in (1, 3, 2)]
    start(loss_copies[:2])
    settle_all(4, 5)
    loss_part(2)
    start(loss_copies[2:])
    gradients(0, 5)
    arrived(loss_copies)
    f2_out[...] = f1_out[0] + (f1_in[0] + f1_in[1] + f1_in[2])
    copies = stage_x(f2_out, f2_in, f2_send, f2_recv)
    start(copies)
    gradients(5, 6)
    arrived(copies)
    f3_out[...] = functools.reduce(jnp.add, [f2_out[...]] + [f2_in[i] for i in range(7)])
    copies = stage_z(f3_out, f3_in, f3_send, f3_recv)
    start(copies)
    gradients(11, 5)
    arrived(copies)
    everything = f3_out[...] + (f3_in[0] + f3_in[1] + f3_in[2])
    loss_ref[...] = own_terms - everything[0:1]

    keep.wait()
    for copy in pending:
        copy.wait_send()


def exchange(key, label, raw, hidden, head, weight):
    dma = pltpu.SemaphoreType.DMA
    vmem = pltpu.VMEM
    tile, quad = (8, BLK), (NY, 8, BLK)
    scratch = [
        vmem((NX, NZ, NC, 2, 8, BLK), F32),
        vmem((NY, ROWS, OLD * BLK), BF16),
        vmem((OLD, CHUNK, BLK), BF16),
        vmem((ENT, BLK, BLK), BF16),
        vmem((NY * ROWS, D), BF16),
        vmem((D, VN), BF16),
        vmem((NY * ROWS, VN), F32),
        vmem((NY * ROWS, VN), F32),
        vmem((NU, NX, NZ, NC, 2, CHUNK, BLK), BF16),
        vmem((NU, 2, 7, 4, 2, HALF, BLK), BF16),
        vmem((NU, 2, 4, PER, HALF, BLK), BF16),
        vmem((NU, 2, 3, PER, HALF, BLK), BF16),
        vmem((2, 7, 4, 2, 8, BLK), F32),
        vmem((NY, ROWS, BLK), F32),
        vmem((NY * ROWS, BLK), F32),
        vmem((NY * ROWS, BLK), F32),
        vmem((NY * ROWS, BLK), F32),
        vmem((NY * ROWS, BLK), F32),
        vmem(tile, F32), vmem((7,) + tile, F32),
        vmem(tile, F32), vmem((3,) + tile, F32),
        vmem(tile, F32), vmem((3,) + tile, F32),
        vmem(quad, F32), vmem((3,) + quad, F32),
        vmem(quad, F32), vmem((7,) + quad, F32),
        vmem(quad, F32), vmem((3,) + quad, F32),
        vmem(quad, F32), vmem((3,) + tile, F32),
        vmem(tile, F32), vmem((7,) + tile, F32),
        vmem(tile, F32), vmem((3,) + tile, F32),
        dma((5,)), dma((6,)), dma((6,)), dma((2, 7)), dma((2, 7)),
        dma((NU, 2, 7)), dma((NU, 2, 7)), dma((NU, 2, 3)), dma((NU, 2, 3)),
        dma((6,)), dma((6,)), dma((3,)), dma((3,)),
    ]
    for count in (7, 3, 3, 3, 7, 3, 3, 7, 3):
        scratch += [dma((count,)), dma((count,))]
    smem = pl.BlockSpec(memory_space=pltpu.SMEM)
    inside = pl.BlockSpec(memory_space=pltpu.VMEM)
    outside = pl.BlockSpec(memory_space=pl.ANY)
    return pl.pallas_call(
        exchange_kernel,
        out_shape=(
            jax.ShapeDtypeStruct((1, ROWS), F32),
            jax.ShapeDtypeStruct((NY * ROWS, VN), BF16),
            jax.ShapeDtypeStruct((NY * ROWS, D), BF16),
        ),
        in_specs=[smem, inside] + [outside] * 4,
        out_specs=(inside, inside, outside),
        scratch_shapes=scratch,
        compiler_params=pltpu.CompilerParams(
            collective_id=0, has_side_effects=True, vmem_limit_bytes=60 << 20
        ),
        name="exchange",
    )(key, label, raw, hidden, head, weight)


GRAD_ROWS = 1152


def grad_kernel(hidden_ref, grad_ref, out_ref):
    out_ref[...] = lax.dot_general(
        hidden_ref[...], grad_ref[...], (((0,), (0,)), ((), ())), preferred_element_type=F32
    ).astype(BF16)


def head_gradient(hidden, grad):
    return pl.pallas_call(
        grad_kernel,
        grid=(D // GRAD_ROWS,),
        out_shape=jax.ShapeDtypeStruct((D, VN), BF16),
        in_specs=[
            pl.BlockSpec((NY * ROWS, GRAD_ROWS), lambda i: (0, i)),
            pl.BlockSpec((NY * ROWS, VN), lambda i: (0, 0)),
        ],
        out_specs=pl.BlockSpec((GRAD_ROWS, VN), lambda i: (i, 0)),
        compiler_params=pltpu.CompilerParams(vmem_limit_bytes=60 << 20),
        name="head_gradient",
    )(hidden, grad)


def local(teacher_logits, hidden, new_head, labels, map_target, map_weight):
    y = lax.axis_index("tok")
    nodes = NX * NZ * NC
    flat = map_target.reshape(1, ENT)
    owner = flat // PER - y * nodes
    match = owner == jnp.arange(nodes, dtype=jnp.int32)[:, None]
    index = jnp.arange(ENT, dtype=jnp.int32)[None, :]
    key = index * PER + flat % PER
    none = ENT * PER
    first = jnp.min(jnp.where(match, key, none), axis=1)
    last = jnp.max(jnp.where(match, key, -1), axis=1)
    first = jnp.where(first < none, first, -1)
    keys = jnp.stack([first, jnp.where(last > first, last, -1)], axis=1).reshape(2 * nodes)
    loss, grad, everyone = exchange(
        keys, labels.reshape(NY, ROWS), teacher_logits, hidden, new_head,
        map_weight.reshape(ENT, BLK, BLK),
    )
    return loss.reshape(ROWS), head_gradient(everyone, grad)


def solution(mesh):
    return jax.shard_map(
        local,
        mesh=mesh,
        in_specs=(
            P("tok", "vocab"),
            P("tok", None),
            P(None, ("tok", "vocab")),
            P(),
            P("vocab", None),
            P("vocab", None, None, None),
        ),
        out_specs=(P("tok"), P(None, ("tok", "vocab"))),
        check_vma=False,
    )
```

time: 139 us -> 121 us (0.87)
  Pallas kernels: 128 us -> 118 us
  local copies, waits for them, and re-layouts: 8.88 us -> 2.09 us
    pallas_call x1, Pallas kernels: 120 us -> 108 us  [exchange(): pl.pallas_call(exchange_kernel, out_shape=(jax.ShapeDtypeStruct((1, ROWS)...]
    unnamed x8 -> x4, local copies, waits for them, and re-layouts: 4.83 us -> 1.28 us
    broadcast_in_dim x2 -> x0, local copies, waits for them, and re-layouts: 2.36 us -> none  [the longest x1 1.53 us: local(): label = jnp.broadcast_to(labels[:, None], (NY * ROWS, BLK))]
where the time goes in v2:
time: 121 us; the launch traced here: 120 us
  Pallas kernels  118 us (98%)
  local copies, waits for them, and re-layouts  2.09 us (2%)
    pallas_call x1, Pallas kernels, exchange(): pl.pallas_call(exchange_kernel, out_shape=(jax.ShapeDtypeStruct((1, ROWS)...  108 us
    pallas_call x1, Pallas kernels, head_gradient(): pl.pallas_call(grad_kernel, grid=(D // GRAD_ROWS,), out_shape=jax.ShapeDt...  9.49 us

profile of v2, /device:TPU:1, one launch (start us, length us, event | category | flops | bytes accessed | tf_op | source)
XLA Modules:
  0.0 120.5 jit_solution(12952802736439448122)
XLA Ops:
  0.6 0.8 copy.12
  1.4 0.1 reshape.139
  1.5 0.1 select_reduce_fusion.1
  1.7 0.1 copy.13
  1.8 0.6 reshape.140.key_ref
  2.4 108.1 %exchange.1 = (f32[1,128]{1,0:T(1,128)}, bf16[512,1024]{1,0:T(8,128)(2,1)}, bf16[512,4608]{1,0:T(8,128)(2,1)}) custom-call(s32[64]{0:T(128)} %reshape.140.key_ref, s32[4,128]{1,0:T(4,128)} %bitcast.10, bf16[128,4096]{1,0:T(8,128)(2,1)} %raw_hbm.1, bf16[128,4608]{1,0:T(8,128)(2,1)} %hidden_hbm.1, bf16[4608,1024]{1,0:T(8,128)(2,1)} %head_hbm.1, ...), custom_call_target="tpu_custom_call" | custom-call | tf_op jit(solution)/shard_map/exchange/pallas_call | solution.py:510
  110.5 0.0 copy-start
  110.5 9.5 %head_gradient.1 = bf16[4608,1024]{1,0:T(8,128)(2,1)} custom-call(bf16[512,4608]{1,0:T(8,128)(2,1)} %get-tuple-element.6.hidden_ref, bf16[512,1024]{1,0:T(8,128)(2,1)} %get-tuple-element.7.grad_ref), custom_call_target="tpu_custom_call" | custom-call | tf_op jit(solution)/shard_map/head_gradient/pallas_call | solution.py:537
  120.0 0.0 copy-done
  120.0 0.5 copy.15
  (3 shorter events, 0.0 us)
Async XLA Ops:
  110.5 9.5 %copy-start = (f32[1,128]{1,0:T(1,128)S(1)}, f32[1,128]{1,0:T(1,128)}, u32[]{:S(2)}) copy-start(f32[1,128]{1,0:T(1,128)} %get-tuple-element.5) | copy-start | bytes 1540

commit v3 on v2

--- a/solution.py
+++ b/solution.py
@@ -17,8 +17,8 @@
 NC = 2
 ROWS = 128
 CHUNK = 64
-HALF = CHUNK // 2
-NU = NY * ROWS // CHUNK
+UNITS = [((0, 0), (0, 1)), ((1, 0), (3, 1)), ((1, 1), (3, 0)), ((2, 0), (2, 1))]
+NU = len(UNITS)
 BLK = 128
 FAN = 4
 D = 4608
@@ -47,7 +47,7 @@
     key_ref, label_ref, raw_hbm, hidden_hbm, head_hbm, weight_hbm,
     loss_ref, grad_ref, everyone_hbm,
     mask_ref, raw, prob, weight, hidden, head, logits, target, out1, in1, out2, in2, masks, mass_acc,
-    log_total, mass_plus, label_at, rest,
+    log_total, mass_plus, label_at, rest, settled,
     t1_out, t1_in, t2_out, t2_in, t3_out, t3_in,
     a1_out, a1_in, a2_out, a2_in, a3_out, a3_in,
     f1_out, f1_in, f2_out, f2_in, f3_out, f3_in,
@@ -110,7 +110,7 @@
     def first_copy(u, h, i):
         da, dc = FIRST[i]
         c2 = (c + dc) % NC
-        rows = pl.ds(h * HALF, HALF)
+        rows = pl.ds(h * CHUNK, CHUNK)
         if h == 0:
             src = out1.at[u, (x + da) % NX, :, c2, :, rows]
         else:
@@ -230,19 +230,20 @@
     start(t3_copies)
     load_weight.wait()
 
-    def contribute(g, part):
-        u = g * 2 + part
-        tokens = pl.ds(part * CHUNK, CHUNK)
-        stats = t3_out[...] if g == 0 else t3_in[g - 1]
-        best = as_column(stats[0:1])[part * CHUNK : (part + 1) * CHUNK]
-        inverse = as_column(1.0 / stats[1:2])[part * CHUNK : (part + 1) * CHUNK]
-
-        def normalise(j, carry):
-            scores = raw[g, tokens, pl.ds(pl.multiple_of(j * BLK, BLK), BLK)].astype(F32)
-            prob[j] = (jnp.exp(scores - best) * inverse).astype(BF16)
-            return carry
-
-        lax.fori_loop(0, OLD, normalise, 0, unroll=4)
+    def contribute(u):
+        for h, (g, part) in enumerate(UNITS[u]):
+            tokens = pl.ds(part * CHUNK, CHUNK)
+            into = pl.ds(h * CHUNK, CHUNK)
+            stats = t3_out[...] if g == 0 else t3_in[g - 1]
+            best = as_column(stats[0:1])[part * CHUNK : (part + 1) * CHUNK]
+            inverse = as_column(1.0 / stats[1:2])[part * CHUNK : (part + 1) * CHUNK]
+
+            def normalise(j, carry):
+                scores = raw[g, tokens, pl.ds(pl.multiple_of(j * BLK, BLK), BLK)].astype(F32)
+                prob[j, into] = (jnp.exp(scores - best) * inverse).astype(BF16)
+                return carry
+
+            lax.fori_loop(0, OLD, normalise, 0, unroll=4)
 
         def slot(o, acc):
             for k in range(2):
@@ -255,20 +256,22 @@
                 acc = acc + product.astype(F32) * filled
             return acc
 
-        acc = lax.fori_loop(0, 32, slot, jnp.zeros((CHUNK, BLK), F32), unroll=4)
-        mass_acc[g, tokens] = acc
+        acc = lax.fori_loop(0, 32, slot, jnp.zeros((2 * CHUNK, BLK), F32), unroll=2)
+        for h, (g, part) in enumerate(UNITS[u]):
+            mass_acc[g, pl.ds(part * CHUNK, CHUNK)] = acc[h * CHUNK : (h + 1) * CHUNK]
         start([first_copy(u, h, i) for i in range(7) for h in (0, 1)])
 
     def merge(u, h):
         arrived([first_copy(u, h, i) for i in range(7)])
-        own = pl.ds(h * HALF, HALF)
-
-        def piece(q, carry):
-            sums = [jnp.zeros((HALF, BLK), F32) for _ in range(PER)]
+
+        def piece(t, carry):
+            q, rows = t // 2, pl.ds(pl.multiple_of((t % 2) * 32, 32), 32)
+            own = pl.ds(pl.multiple_of(h * CHUNK + (t % 2) * 32, 32), 32)
+            sums = [jnp.zeros((32, BLK), F32) for _ in range(PER)]
             for i in range(8):
                 for k in range(2):
                     if i < 7:
-                        part, hit = in1[u, h, i, q, k], masks[h, i, q, k]
+                        part, hit = in1[u, h, i, q, k, rows], masks[h, i, q, k]
                     elif h == 0:
                         part, hit = out1[u, x, q, c, k, own], mask_ref[x, q, c, k]
                     else:
@@ -277,10 +280,10 @@
                     for b in range(PER):
                         sums[b] = sums[b] + part * hit[b : b + 1]
             for b in range(PER):
-                out2[u, h, q, b] = sums[b].astype(BF16)
+                out2[u, h, q, b, rows] = sums[b].astype(BF16)
             return carry
 
-        lax.fori_loop(0, 4, piece, 0)
+        lax.fori_loop(0, 8, piece, 0)
         start([second_copy(u, h, d) for d in (1, 2, 3)])
 
     def merge_all(*units):
@@ -290,7 +293,7 @@
 
     def group_rows(g, first=0, count=ROWS):
         start_row = ((y - g + NY) % NY) * ROWS + first
-        return pl.ds(pl.multiple_of(start_row, HALF), count)
+        return pl.ds(pl.multiple_of(start_row, CHUNK), count)
 
     def student(g):
         rows = group_rows(g)
@@ -321,26 +324,34 @@
         return jnp.where(sublane == 0, wide[0], jnp.where(sublane == 1, wide[1], wide[2]))
 
     base = (y * (NX * NZ * NC) + v) * VN
-    lane = (lax.broadcasted_iota(jnp.int32, (HALF, BLK), 1) + base).astype(F32)
+    lane = (lax.broadcasted_iota(jnp.int32, (32, BLK), 1) + base).astype(F32)
     for q in range(NY):
         label_at[pl.ds(q * ROWS, ROWS)] = as_column(label_ref[pl.ds(q, 1)].astype(F32))
 
     def settle(u, h):
         arrived([second_copy(u, h, d) for d in (1, 2, 3)])
         q = z if h == 0 else x
-        rows = group_rows(u // 2, (u % 2) * CHUNK + h * HALF, HALF)
-        label_here = label_at[rows]
-        acc = jnp.zeros((HALF, BLK), F32)
-        for b in range(PER):
-            here = out2[u, h, q, b].astype(F32)
-            for d in range(3):
-                here = here + in2[u, h, d, b].astype(F32)
-            columns = pl.ds(b * BLK, BLK)
-            hit = (label_here == lane + float(b * BLK)).astype(F32)
-            here = here + hit
-            target[rows, columns] = here
-            acc = acc + here * logits[rows, columns]
-        rest[rows] = acc
+        g, half = UNITS[u][h]
+
+        def piece(t, carry):
+            part = pl.ds(pl.multiple_of(t * 32, 32), 32)
+            start_row = ((y - g + NY) % NY) * ROWS + half * CHUNK + t * 32
+            rows = pl.ds(pl.multiple_of(start_row, 32), 32)
+            label_here = label_at[rows]
+            acc = jnp.zeros((32, BLK), F32)
+            for b in range(PER):
+                here = out2[u, h, q, b, part].astype(F32)
+                for d in range(3):
+                    here = here + in2[u, h, d, b, part].astype(F32)
+                columns = pl.ds(b * BLK, BLK)
+                hit = (label_here == lane + float(b * BLK)).astype(F32)
+                here = here + hit
+                target[rows, columns] = here
+                acc = acc + here * logits[rows, columns]
+            rest[rows] = acc
+            return carry
+
+        lax.fori_loop(0, CHUNK // 32, piece, 0)
 
     def settle_all(*units):
         for u in units:
@@ -377,34 +388,32 @@
         return remote(f1_out.at[g], f1_in.at[g - 1], f1_send.at[g - 1], f1_recv.at[g - 1],
                       along_y(NY - g))
 
-    contribute(0, 0)
-    contribute(0, 1)
+    contribute(0)
     arrived(raw_copies[0:2])
     start(raw_copies[2:4])
     arrived(t3_copies)
-    contribute(1, 0)
-    contribute(3, 1)
+    contribute(1)
     arrived(mask_copies)
-    merge_all(0, 1)
+    merge_all(0)
     arrived(raw_copies[2:4])
     start(raw_copies[4:6])
-    contribute(1, 1)
-    contribute(3, 0)
+    contribute(2)
     load_hidden.wait()
     load_head.wait()
-    merge_all(2, 7)
+    merge_all(1)
     arrived(raw_copies[4:6])
     start(hidden_copies[0:4])
-    contribute(2, 0)
-    contribute(2, 1)
+    contribute(3)
     student(0)
-    merge_all(3, 6)
+    merge_all(2)
     arrived(hidden_copies[0:4])
     start(hidden_copies[4:6])
     sibling_copies = [sibling_copy(d) for d in (1, 3, 2)]
     start(sibling_copies[:2])
+    settle_all(0)
     arrived(sibling_copies[:2])
     student(1)
+    merge_all(3)
     student(3)
     arrived(hidden_copies[4:6])
     start(sibling_copies[2:])
@@ -415,37 +424,34 @@
 
     copies = stage_y(a1_out, a1_in, a1_send, a1_recv)
     start(copies)
-    settle_all(0, 1)
+    settle_all(1)
     arrived(copies)
     combine(a2_out, a1_out, a1_in, 3)
     copies = stage_x(a2_out, a2_in, a2_send, a2_recv)
     start(copies)
-    merge_all(4)
+    settle_all(2)
+    for g in (0, 1, 3):
+        loss_part(g)
+    loss_copies = [loss_copy(g) for g in (1, 3, 2)]
+    start(loss_copies[:2])
     arrived(copies)
     combine(a3_out, a2_out, a2_in, 7)
     copies = stage_z(a3_out, a3_in, a3_send, a3_recv)
     start(copies)
-    merge_all(5)
-    settle_all(2, 7)
+    settle_all(3)
+    loss_part(2)
+    start(loss_copies[2:])
     arrived(copies)
     for q in range(NY):
         stats = joined3([a3_out[q]] + [a3_in[i, q] for i in range(3)])
         rows = pl.ds(q * ROWS, ROWS)
         log_total[rows] = as_column(stats[0:1] + jnp.log(stats[1:2]))
         mass_plus[rows] = as_column(stats[2:3] + 1.0)
-        f1_out[q] = stats
-
-    mine = f1_out[y]
+        settled[q] = stats
+
+    mine = settled[y]
     own_log = mine[0:1] + jnp.log(mine[1:2])
     own_terms = mine[2:3] * own_log + own_log
-    settle_all(3, 6)
-    for g in (0, 1, 3):
-        loss_part(g)
-    loss_copies = [loss_copy(g) for g in (1, 3, 2)]
-    start(loss_copies[:2])
-    settle_all(4, 5)
-    loss_part(2)
-    start(loss_copies[2:])
     gradients(0, 5)
     arrived(loss_copies)
     f2_out[...] = f1_out[0] + (f1_in[0] + f1_in[1] + f1_in[2])
@@ -473,22 +479,23 @@
     scratch = [
         vmem((NX, NZ, NC, 2, 8, BLK), F32),
         vmem((NY, ROWS, OLD * BLK), BF16),
-        vmem((OLD, CHUNK, BLK), BF16),
+        vmem((OLD, 2 * CHUNK, BLK), BF16),
         vmem((ENT, BLK, BLK), BF16),
         vmem((NY * ROWS, D), BF16),
         vmem((D, VN), BF16),
         vmem((NY * ROWS, VN), F32),
         vmem((NY * ROWS, VN), F32),
-        vmem((NU, NX, NZ, NC, 2, CHUNK, BLK), BF16),
-        vmem((NU, 2, 7, 4, 2, HALF, BLK), BF16),
-        vmem((NU, 2, 4, PER, HALF, BLK), BF16),
-        vmem((NU, 2, 3, PER, HALF, BLK), BF16),
+        vmem((NU, NX, NZ, NC, 2, 2 * CHUNK, BLK), BF16),
+        vmem((NU, 2, 7, 4, 2, CHUNK, BLK), BF16),
+        vmem((NU, 2, 4, PER, CHUNK, BLK), BF16),
+        vmem((NU, 2, 3, PER, CHUNK, BLK), BF16),
         vmem((2, 7, 4, 2, 8, BLK), F32),
         vmem((NY, ROWS, BLK), F32),
         vmem((NY * ROWS, BLK), F32),
         vmem((NY * ROWS, BLK), F32),
         vmem((NY * ROWS, BLK), F32),
         vmem((NY * ROWS, BLK), F32),
+        vmem(quad, F32),
         vmem(tile, F32), vmem((7,) + tile, F32),
         vmem(tile, F32), vmem((3,) + tile, F32),
         vmem(tile, F32), vmem((3,) + tile, F32),

time: 121 us -> 125 us (1.033)
  Pallas kernels: 118 us -> 122 us
    pallas_call x1, Pallas kernels: 108 us -> 112 us  [exchange(): pl.pallas_call(exchange_kernel, out_shape=(jax.ShapeDtypeStruct((1, ROWS)...]
where the time goes in v3:
time: 125 us
  Pallas kernels  122 us (98%)
  local copies, waits for them, and re-layouts  2.09 us (2%)
    pallas_call x1, Pallas kernels, exchange(): pl.pallas_call(exchange_kernel, out_shape=(jax.ShapeDtypeStruct((1, ROWS)...  112 us
    pallas_call x1, Pallas kernels, head_gradient(): pl.pallas_call(grad_kernel, grid=(D // GRAD_ROWS,), out_shape=jax.ShapeDt...  9.49 us

profile of v3, /device:TPU:1, one launch (start us, length us, event | category | flops | bytes accessed | tf_op | source)
XLA Modules:
  0.0 124.9 jit_solution(4258693207201049901)
XLA Ops:
  0.6 0.8 copy.12
  1.4 0.1 reshape.139
  1.5 0.1 select_reduce_fusion.1
  1.7 0.1 copy.13
  1.8 0.6 reshape.140.key_ref
  2.4 112.5 %exchange.1 = (f32[1,128]{1,0:T(1,128)}, bf16[512,1024]{1,0:T(8,128)(2,1)}, bf16[512,4608]{1,0:T(8,128)(2,1)}) custom-call(s32[64]{0:T(128)} %reshape.140.key_ref, s32[4,128]{1,0:T(4,128)} %bitcast.10, bf16[128,4096]{1,0:T(8,128)(2,1)} %raw_hbm.1, bf16[128,4608]{1,0:T(8,128)(2,1)} %hidden_hbm.1, bf16[4608,1024]{1,0:T(8,128)(2,1)} %head_hbm.1, ...), custom_call_target="tpu_custom_call" | custom-call | tf_op jit(solution)/shard_map/exchange/pallas_call | solution.py:517
  114.9 0.0 copy-start
  114.9 9.5 %head_gradient.1 = bf16[4608,1024]{1,0:T(8,128)(2,1)} custom-call(bf16[512,4608]{1,0:T(8,128)(2,1)} %get-tuple-element.6.hidden_ref, bf16[512,1024]{1,0:T(8,128)(2,1)} %get-tuple-element.7.grad_ref), custom_call_target="tpu_custom_call" | custom-call | tf_op jit(solution)/shard_map/head_gradient/pallas_call | solution.py:544
  124.4 0.0 copy-done
  124.4 0.5 copy.15
  (3 shorter events, 0.0 us)
Async XLA Ops:
  114.9 9.5 %copy-start = (f32[1,128]{1,0:T(1,128)S(1)}, f32[1,128]{1,0:T(1,128)}, u32[]{:S(2)}) copy-start(f32[1,128]{1,0:T(1,128)} %get-tuple-element.5) | copy-start | bytes 1540

commit v4 on v2

--- a/solution.py
+++ b/solution.py
@@ -186,14 +186,11 @@
             mask_ref[o // (NZ * NC), (o // NC) % NZ, o % NC, k] = (sublane == row).astype(F32)
         return carry
 
-    lax.fori_loop(0, NX * NZ * NC, mask_rows, 0, unroll=4)
     load_raw.wait()
     start(raw_copies[:2])
     load_weight.start()
     load_hidden.start()
     load_head.start()
-    mask_copies = [mask_copy(h, i) for h in (0, 1) for i in range(7)]
-    start(mask_copies)
 
     def block_max(j, acc):
         part = raw[0, :, pl.ds(pl.multiple_of(j * BLK, BLK), BLK)].astype(F32)
@@ -220,6 +217,9 @@
     t1_out[...] = stacked(as_row(top[:, 0:1]), as_row(total))
     copies = stage_x(t1_out, t1_in, t1_send, t1_recv)
     start(copies)
+    lax.fori_loop(0, NX * NZ * NC, mask_rows, 0, unroll=4)
+    mask_copies = [mask_copy(h, i) for h in (0, 1) for i in range(7)]
+    start(mask_copies)
     arrived(copies)
     t2_out[...] = joined([t1_out[...]] + [t1_in[i] for i in range(7)])
     copies = stage_z(t2_out, t2_in, t2_send, t2_recv)
@@ -322,8 +322,6 @@
 
     base = (y * (NX * NZ * NC) + v) * VN
     lane = (lax.broadcasted_iota(jnp.int32, (HALF, BLK), 1) + base).astype(F32)
-    for q in range(NY):
-        label_at[pl.ds(q * ROWS, ROWS)] = as_column(label_ref[pl.ds(q, 1)].astype(F32))
 
     def settle(u, h):
         arrived([second_copy(u, h, d) for d in (1, 2, 3)])
@@ -397,6 +395,8 @@
     start(hidden_copies[0:4])
     contribute(2, 0)
     contribute(2, 1)
+    for q in range(NY):
+        label_at[pl.ds(q * ROWS, ROWS)] = as_column(label_ref[pl.ds(q, 1)].astype(F32))
     student(0)
     merge_all(3, 6)
     arrived(hidden_copies[0:4])
@@ -524,7 +524,7 @@
     )(key, label, raw, hidden, head, weight)
 
 
-GRAD_ROWS = 1152
+GRAD_ROWS = 1536
 
 
 def grad_kernel(hidden_ref, grad_ref, out_ref):

time: 121 us -> 119 us (0.983)
  Pallas kernels: 118 us -> 116 us
    pallas_call x1, Pallas kernels: 108 us -> 107 us  [exchange(): pl.pallas_call(exchange_kernel, out_shape=(jax.ShapeDtypeStruct((1, ROWS)...]
where the time goes in v4:
time: 119 us
  Pallas kernels  116 us (97%)
  local copies, waits for them, and re-layouts  2.09 us (2%)
    pallas_call x1, Pallas kernels, exchange(): pl.pallas_call(exchange_kernel, out_shape=(jax.ShapeDtypeStruct((1, ROWS)...  107 us
    pallas_call x1, Pallas kernels, head_gradient(): pl.pallas_call(grad_kernel, grid=(D // GRAD_ROWS,), out_shape=jax.ShapeDt...  9.59 us

profile of v4, /device:TPU:1, one launch (start us, length us, event | category | flops | bytes accessed | tf_op | source)
XLA Modules:
  0.0 119.0 jit_solution(6329790887450651346)
XLA Ops:
  0.6 0.8 copy.12
  1.4 0.1 reshape.139
  1.5 0.1 select_reduce_fusion.1
  1.7 0.1 copy.13
  1.8 0.6 reshape.140.key_ref
  2.4 106.5 %exchange.1 = (f32[1,128]{1,0:T(1,128)}, bf16[512,1024]{1,0:T(8,128)(2,1)}, bf16[512,4608]{1,0:T(8,128)(2,1)}) custom-call(s32[64]{0:T(128)} %reshape.140.key_ref, s32[4,128]{1,0:T(4,128)} %bitcast.10, bf16[128,4096]{1,0:T(8,128)(2,1)} %raw_hbm.1, bf16[128,4608]{1,0:T(8,128)(2,1)} %hidden_hbm.1, bf16[4608,1024]{1,0:T(8,128)(2,1)} %head_hbm.1, ...), custom_call_target="tpu_custom_call" | custom-call | tf_op jit(solution)/shard_map/exchange/pallas_call | solution.py:510
  108.9 0.0 copy-start
  108.9 9.6 %head_gradient.1 = bf16[4608,1024]{1,0:T(8,128)(2,1)} custom-call(bf16[512,4608]{1,0:T(8,128)(2,1)} %get-tuple-element.6.hidden_ref, bf16[512,1024]{1,0:T(8,128)(2,1)} %get-tuple-element.7.grad_ref), custom_call_target="tpu_custom_call" | custom-call | tf_op jit(solution)/shard_map/head_gradient/pallas_call | solution.py:537
  118.5 0.0 copy-done
  118.5 0.5 copy.15
  (3 shorter events, 0.0 us)
Async XLA Ops:
  108.9 9.6 %copy-start = (f32[1,128]{1,0:T(1,128)S(1)}, f32[1,128]{1,0:T(1,128)}, u32[]{:S(2)}) copy-start(f32[1,128]{1,0:T(1,128)} %get-tuple-element.5) | copy-start | bytes 1540

commit v5 on v4

--- a/solution.py
+++ b/solution.py
@@ -390,9 +390,9 @@
     contribute(3, 0)
     load_hidden.wait()
     load_head.wait()
+    start(hidden_copies[0:4])
     merge_all(2, 7)
     arrived(raw_copies[4:6])
-    start(hidden_copies[0:4])
     contribute(2, 0)
     contribute(2, 1)
     for q in range(NY):

time: 119 us -> 119 us (level)
  no operation moved by 1% of the time
where the time goes in v5:
time: 119 us
  Pallas kernels  116 us (97%)
  local copies, waits for them, and re-layouts  2.09 us (2%)
    pallas_call x1, Pallas kernels, exchange(): pl.pallas_call(exchange_kernel, out_shape=(jax.ShapeDtypeStruct((1, ROWS)...  106 us
    pallas_call x1, Pallas kernels, head_gradient(): pl.pallas_call(grad_kernel, grid=(D // GRAD_ROWS,), out_shape=jax.ShapeDt...  9.59 us

profile of v5, /device:TPU:1, one launch (start us, length us, event | category | flops | bytes accessed | tf_op | source)
XLA Modules:
  0.0 119.0 jit_solution(8893946148471800982)
XLA Ops:
  0.6 0.8 copy.12
  1.4 0.1 reshape.139
  1.5 0.1 select_reduce_fusion.1
  1.7 0.1 copy.13
  1.8 0.6 reshape.140.key_ref
  2.4 106.5 %exchange.1 = (f32[1,128]{1,0:T(1,128)}, bf16[512,1024]{1,0:T(8,128)(2,1)}, bf16[512,4608]{1,0:T(8,128)(2,1)}) custom-call(s32[64]{0:T(128)} %reshape.140.key_ref, s32[4,128]{1,0:T(4,128)} %bitcast.10, bf16[128,4096]{1,0:T(8,128)(2,1)} %raw_hbm.1, bf16[128,4608]{1,0:T(8,128)(2,1)} %hidden_hbm.1, bf16[4608,1024]{1,0:T(8,128)(2,1)} %head_hbm.1, ...), custom_call_target="tpu_custom_call" | custom-call | tf_op jit(solution)/shard_map/exchange/pallas_call | solution.py:510
  108.8 0.0 copy-start
  108.9 9.6 %head_gradient.1 = bf16[4608,1024]{1,0:T(8,128)(2,1)} custom-call(bf16[512,4608]{1,0:T(8,128)(2,1)} %get-tuple-element.6.hidden_ref, bf16[512,1024]{1,0:T(8,128)(2,1)} %get-tuple-element.7.grad_ref), custom_call_target="tpu_custom_call" | custom-call | tf_op jit(solution)/shard_map/head_gradient/pallas_call | solution.py:537
  118.4 0.0 copy-done
  118.4 0.5 copy.15
  (3 shorter events, 0.0 us)
Async XLA Ops:
  108.8 9.6 %copy-start = (f32[1,128]{1,0:T(1,128)S(1)}, f32[1,128]{1,0:T(1,128)}, u32[]{:S(2)}) copy-start(f32[1,128]{1,0:T(1,128)} %get-tuple-element.5) | copy-start | bytes 1540
